TPU v7x, 128 devices: a whole 4x4x4 slice. The times are simulated.
128 devices in a mesh: rep: 8 (over x, z_hi), tp: 16 (over z_lo, y, core).
Axes of the slice: x: 4, y: 4, z: 4 (z_hi: 2, z_lo: 2; z = z_hi * 2 + z_lo), core: 2. Of those that a mesh axis runs over, the one named last changes fastest.
Arguments:
- hidden_in: bfloat16 [8192, 8192], P('rep'), may hold values from -6 to 6
- norm_gain: float32 [8192], replicated, may hold values from 0.1 to 1.9
- w_query: bfloat16 [8192, 8192], P(('rep', 'tp'))
- w_keyval: bfloat16 [8192, 2048], P(('rep', 'tp'))
- w_out: bfloat16 [8192, 8192], P(None, ('rep', 'tp')), may hold values from -0.25 to 0.25
- doc_lengths: int32 [8, 4], P('rep'), may hold values from 1 to 512, 1024 in all within a row
Outputs:
- mixed: bfloat16 [8192, 8192], P(('rep', 'tp'))
Inputs may be any that keep to these rules, and one draw needn't show every extreme that they name: `doc_lengths`: each replica's lengths sum to 1024, and the longest has exactly 512 tokens.
All inputs are finite; a program needn't handle non-finite values.
Results may differ from a plain program's by a relative error of at most 0.023.
The roundings to bfloat16 on the way count: a program that leaves them out, or rounds other values in their place, can miss the bound.
Values may be sent and summed in bfloat16 or wider, within the bound.
No kernel may reach another device: no remote copies, remote signals or barrier semaphores. Data moves between devices by JAX's collectives and lax.ppermute only.
A program may use at most 192 MiB of HBM per device.

v0:
```python
import jax
import jax.numpy as jnp
from jax import lax
from jax.sharding import PartitionSpec as P

H = 64
KVH = 8
HD = 128


theta_base = 1000000.0
eps_norm = 1e-06


def rotary(tensor, positions):
    half = tensor.shape[-1] // 2
    freqs = theta_base ** (-(jnp.arange(half, dtype=jnp.float32) * 2.0 / tensor.shape[-1]))
    angles = positions.astype(jnp.float32)[:, None] * freqs[None, :]
    cosine = jnp.cos(angles)[:, None, :]
    sine = jnp.sin(angles)[:, None, :]
    first = tensor[..., :half]
    second = tensor[..., half:]
    return jnp.concatenate(
        [first * cosine - second * sine, second * cosine + first * sine], axis=-1
    )


def doc_layout(lengths, count):
    places = jnp.arange(count, dtype=jnp.int32)
    ends = jnp.cumsum(lengths)
    after = places[:, None] >= ends[None, :]
    segment = jnp.sum(after.astype(jnp.int32), axis=1)
    starts = jnp.sum(jnp.where(after, lengths[None, :], 0), axis=1)
    return (places, segment, places - starts)


def attend(query, keys, values, places, segment):
    count = query.shape[0]
    block = min(count, 512)
    scale = keys.shape[-1] ** (-0.5)

    def one_block(number):
        begin = number * block
        rows = lax.dynamic_slice_in_dim(query, begin, block, 0)
        row_place = lax.dynamic_slice_in_dim(places, begin, block, 0)
        row_seg = lax.dynamic_slice_in_dim(segment, begin, block, 0)
        scores = jnp.einsum("qgd,kd->gqk", rows, keys, preferred_element_type=jnp.float32) * scale
        allowed = (row_seg[:, None] == segment[None, :]) & (places[None, :] <= row_place[:, None])
        scores = jnp.where(allowed[None], scores, -1e30)
        top = jnp.max(scores, axis=-1, keepdims=True)
        weights = jnp.exp(scores - top)
        probs = (weights / jnp.sum(weights, axis=-1, keepdims=True)).astype(jnp.bfloat16)
        blended = jnp.einsum("gqk,kd->qgd", probs, values, preferred_element_type=jnp.float32)
        return blended.astype(jnp.bfloat16).reshape(block, -1)

    numbers = jnp.arange(count // block, dtype=jnp.int32)
    return lax.map(one_block, numbers).reshape(count, -1)


def pack_columns(query_rows, keyval_rows, tp_count):
    row_count = query_rows.shape[0]
    query_part = query_rows.reshape(row_count, tp_count, -1)
    keyval_part = keyval_rows.reshape(row_count, 2, KVH, HD)
    keyval_part = jnp.repeat(keyval_part, tp_count // KVH, axis=2)
    keyval_part = keyval_part.transpose(0, 2, 1, 3).reshape(row_count, tp_count, 2 * HD)
    return jnp.concatenate([query_part, keyval_part], axis=2).reshape(row_count, -1)


def shards(hidden_in, norm_gain, w_query, w_keyval, w_out, doc_lengths):
    tp_count = lax.axis_size("tp")
    token_count = hidden_in.shape[0]
    heads_here = H // tp_count
    packed = pack_columns(w_query, w_keyval, tp_count)
    sliced = lax.all_to_all(packed, "tp", split_axis=1, concat_axis=0, tiled=True)
    out_sliced = lax.all_to_all(w_out, "tp", split_axis=0, concat_axis=1, tiled=True)
    floats = hidden_in.astype(jnp.float32)
    power = jnp.mean(floats * floats, axis=-1, keepdims=True)
    normed = (floats * lax.rsqrt(power + eps_norm) * norm_gain[None, :]).astype(jnp.bfloat16)
    w_columns = lax.all_gather(sliced, "rep", axis=0, tiled=True)
    projected = jnp.dot(normed, w_columns, preferred_element_type=jnp.float32)
    w_rows = lax.all_gather(out_sliced, "rep", axis=1, tiled=True)
    query_width = heads_here * HD
    query = projected[:, :query_width].reshape(token_count, heads_here, HD)
    keys = projected[:, query_width : query_width + HD].reshape(token_count, 1, HD)
    values = projected[:, query_width + HD :].astype(jnp.bfloat16)
    places, segment, positions = doc_layout(doc_lengths[0], token_count)
    query_rot = rotary(query, positions).astype(jnp.bfloat16)
    key_rot = rotary(keys, positions).astype(jnp.bfloat16)[:, 0]
    context = attend(query_rot, key_rot, values, places, segment)
    share = token_count // tp_count
    summed = lax.psum_scatter(
        jnp.dot(context, w_rows, preferred_element_type=jnp.float32).astype(jnp.bfloat16),
        "tp",
        scatter_dimension=0,
        tiled=True,
    ).astype(jnp.float32)
    own_rows = lax.dynamic_slice_in_dim(floats, lax.axis_index("tp") * share, share, 0)
    return (own_rows + summed).astype(jnp.bfloat16)


def solution(mesh):
    in_specs = (
        P("rep", None),
        P(),
        P(("rep", "tp"), None),
        P(("rep", "tp"), None),
        P(None, ("rep", "tp")),
        P("rep", None),
    )
    out_specs = P(("rep", "tp"), None)
    return jax.shard_map(shards, mesh=mesh, in_specs=in_specs, out_specs=out_specs, check_vma=False)
```

profile of v0, /device:TPU:0, one launch (start us, length us, event | category | flops | bytes accessed | tf_op | source)
XLA Modules:
  0.0 419.9 jit_solution(228208639149454164)
XLA Ops:
  8.5 1.6 copy.42
  10.6 28.0 %all_to_all.35 = bf16[64,16,768]{2,0,1:T(8,128)(2,1)} all-to-all(bf16[64,16,768]{2,0,1:T(8,128)(2,1)S(1)} %copy.31), channel_id=1, replica_groups=mesh['rep'=8,'tp'=16] {'tp'}, dimensions={1} | all-to-all | bytes 3145728 | tf_op jit(solution)/shard_map/all_to_all | solution.py:74
  38.9 19.8 %all_to_all.36 = bf16[16,512,64]{1,2,0:T(8,128)(2,1)} all-to-all(bf16[16,512,64]{1,2,0:T(8,128)(2,1)S(1)} %bitcast.76), channel_id=1, replica_groups=mesh['rep'=8,'tp'=16] {'tp'}, dimensions={0} | all-to-all | bytes 2097152 | tf_op jit(solution)/shard_map/all_to_all | solution.py:75
  59.0 7.2 %multiply_reduce_fusion = f32[1024]{0:T(1024)S(1)} fusion(bf16[1024,8192]{1,0:T(8,128)(2,1)} %param.8), kind=kLoop, calls=%fused_computation.26 | loop fusion | flops 25164800 | bytes 16781312 | tf_op jit(solution)/shard_map/reduce_sum | solution.py:77
  66.3 3.1 multiply_cosine_fusion
  69.4 120.8 %all-gather.3.cloned.1.call-done = bf16[8192,768]{1,0:T(8,128)(2,1)} async-done(((bf16[1024,768]{1,0:T(8,128)(2,1)}), bf16[8192,768]{1,0:T(8,128)(2,1)}) %all-gather.3.cloned.1.call-update) | async-done | bytes 12582928 | tf_op jit(solution)/shard_map/all_gather | solution.py:79
  190.2 25.2 %fusion.30 = f32[1024,768]{0,1:T(8,128)S(1)} fusion(bf16[8192,768]{1,0:T(8,128)(2,1)} %all-gather.3.cloned.1.call-done, f32[8192]{0:T(1024)S(1)} %copy-done.4, f32[1024]{0:T(1024)S(1)} %add_rsqrt_fusion, bf16[1024,8192]{1,0:T(8,128)(2,1)} %param.8), kind=kOutput, calls=%fused_computation.27 | convolution fusion | flops 12918456320 | bytes 32542720 | tf_op jit(solution)/shard_map/dot_general | solution.py:80
  215.4 1.7 copy-done
  217.1 1.8 slice.29
  220.0 1.2 fusion.43
  222.1 1.2 fusion.53
  223.3 1.8 copy.40
  225.1 2.0 copy.39
  227.0 2.4 subtract_convert_fusion
  230.1 27.0 %while.11 = (s32[]{:T(128)}, bf16[2,512,512]{2,1,0:T(8,128)(2,1)}, s32[2]{0:T(128)S(1)}, s32[1024]{0:T(1024)S(1)}, s32[1024]{0:T(1024)S(1)}, /*index=5*/bf16[102...) while((s32[]{:T(128)}, bf16[2,512,512]{2,1,0:T(8,128)(2,1)}, ...), condition=%wide.region_7.8_spmd.clone, body=%wide.region_4.7_spmd.clone.sunk | while | flops 1088160768 | bytes 21532872 | solution.py:57
  232.3 5.4 %fusion.65 = (f32[4,512]{1,0:T(4,128)S(1)}, f32[4,512,1024]{2,1,0:T(8,128)}) fusion(pred[512,1024]{1,0:T(8,128)(4,1)S(1)} %compare_and_fusion.2, bf16[1024,4,128]{2,0,1:T(8,128)(2,1)S(1)} %get-tuple-element.221, s32[]{:T(128)S(6)} %select_n.40, bf16[1024,128]{1,0:T(8,128)(2,1)S(1)} %get-tuple-element.222), kind=kOutput, calls=%fused_computation.61.clone.1 | convolution fusion | flops 545260544 | bytes 9707524 | tf_op jit(solution)/shard_map/while/body/eval_jaxpr/sub | solution.py:51
  237.7 5.0 %fusion.66 = bf16[4,512,128]{1,2,0:T(8,128)(2,1)S(1)} fusion(f32[4,512,1024]{2,1,0:T(8,128)} %get-tuple-element.190, f32[4,512]{1,0:T(4,128)S(1)} %get-tuple-element.191, bf16[1024,128]{0,1:T(8,128)(2,1)S(1)} %get-tuple-element.223), kind=kOutput, calls=%fused_computation.12.clone.1 | convolution fusion | flops 541327360 | bytes 9183232 | tf_op jit(solution)/shard_map/while/body/eval_jaxpr/gqk,kd->qgd/dot_general | solution.py:53
  245.7 5.4 %fusion.65 = (f32[4,512]{1,0:T(4,128)S(1)}, f32[4,512,1024]{2,1,0:T(8,128)}) fusion(pred[512,1024]{1,0:T(8,128)(4,1)S(1)} %compare_and_fusion.2, bf16[1024,4,128]{2,0,1:T(8,128)(2,1)S(1)} %get-tuple-element.221, s32[]{:T(128)S(6)} %select_n.40, bf16[1024,128]{1,0:T(8,128)(2,1)S(1)} %get-tuple-element.222), kind=kOutput, calls=%fused_computation.61.clone.1 | convolution fusion | flops 545260544 | bytes 9707524 | tf_op jit(solution)/shard_map/while/body/eval_jaxpr/sub | solution.py:51
  251.1 5.0 %fusion.66 = bf16[4,512,128]{1,2,0:T(8,128)(2,1)S(1)} fusion(f32[4,512,1024]{2,1,0:T(8,128)} %get-tuple-element.190, f32[4,512]{1,0:T(4,128)S(1)} %get-tuple-element.191, bf16[1024,128]{0,1:T(8,128)(2,1)S(1)} %get-tuple-element.223), kind=kOutput, calls=%fused_computation.12.clone.1 | convolution fusion | flops 541327360 | bytes 9183232 | tf_op jit(solution)/shard_map/while/body/eval_jaxpr/gqk,kd->qgd/dot_general | solution.py:53
  257.1 42.1 %all-gather.5.cloned.1.call-done = bf16[512,8192]{0,1:T(8,128)(2,1)} async-done(((bf16[512,1024]{0,1:T(8,128)(2,1)}), bf16[512,8192]{0,1:T(8,128)(2,1)}) %all-gather.5.cloned.1.call-update) | async-done | bytes 8388624 | tf_op jit(solution)/shard_map/all_gather | solution.py:81
  299.2 14.9 %convolution_convert_fusion = bf16[1024,8192]{1,0:T(8,128)(2,1)} fusion(bf16[1024,512]{1,0:T(8,128)(2,1)} %bitcast.85, bf16[512,8192]{0,1:T(8,128)(2,1)} %all-gather.5.cloned.1.call-done), kind=kOutput, calls=%fused_computation.31 | convolution fusion | flops 8598323200 | bytes 26214400 | tf_op jit(solution)/shard_map/dot_general | solution.py:92
  314.1 18.7 %convert_element_type.41 = f32[1024,8192]{1,0:T(8,128)} convert(bf16[1024,8192]{1,0:T(8,128)(2,1)} %param.8) | non-fusion elementwise | flops 8388608 | bytes 50331648 | tf_op jit(solution)/shard_map/convert_element_type | solution.py:76
  332.7 77.6 %reduce-scatter.2.cloned.1.call-done = bf16[64,8192]{1,0:T(8,128)(2,1)} async-done(((bf16[1024,8192]{1,0:T(8,128)(2,1)}), bf16[64,8192]{1,0:T(8,128)(2,1)}) %reduce-scatter.2.cloned.1.call-update) | async-done | bytes 1048592 | tf_op jit(solution)/shard_map/reduce_scatter | solution.py:91
  410.3 3.1 add_convert_fusion
  (47 shorter events, 10.3 us)
Async XLA Ops:
  6.5 32.2 %copy-start.1 = (bf16[8192,64]{0,1:T(8,128)(2,1)S(1)}, bf16[8192,64]{0,1:T(8,128)(2,1)}, u32[]{:S(2)}) copy-start(bf16[8192,64]{0,1:T(8,128)(2,1)} %param.12) | copy-start | bytes 3145732
  6.5 183.6 %all-gather.3.cloned.1.call-start = ((), (), s32[]{:S(2)}) async-start(), calls=%async_computation.3 | async-start | bytes 14155776 | tf_op jit(solution)/shard_map/all_gather | solution.py:79
  10.0 48.7 %copy-start.3 = (s32[1,4]{1,0:T(1,128)S(1)}, s32[1,4]{1,0:T(1,128)}, u32[]{:S(2)}) copy-start(s32[1,4]{1,0:T(1,128)} %param.13) | copy-start | bytes 52
  38.7 260.5 %all-gather.5.cloned.1.call-start = ((), (), s32[]{:S(2)}) async-start(), calls=%async_computation.4 | async-start | bytes 9437184 | tf_op jit(solution)/shard_map/all_gather | solution.py:81
  58.7 351.7 %reduce-scatter.2.cloned.1.call-start = ((), (), s32[]{:S(2)}) async-start(), calls=%async_computation.5 | async-start | bytes 17825792 | tf_op jit(solution)/shard_map/reduce_scatter | solution.py:91
  59.0 131.2 %copy-start.4 = (f32[8192]{0:T(1024)S(1)}, f32[8192]{0:T(1024)}, u32[]{:S(2)}) copy-start(f32[8192]{0:T(1024)} %param.9) | copy-start | bytes 98308
  215.4 1.7 copy-start
  227.0 3.0 copy-start.2
Sparse Core Ops, SparseCore 0:
  38.8 151.3 all-gather.2
  192.5 106.6 all-gather.4
  314.2 96.0 reduce-scatter.1
where the time goes:
time: 421 us; the launch traced here: 420 us
  waiting for transfers between devices  241 us (57%)
  matrix products  60.8 us (14%)
  blocking collectives  47.8 us (11%)
  other arithmetic  37.6 us (9%)
  local copies, waits for them, and re-layouts  18.2 us (4%)
  between operations  13.3 us (3%)
    all_gather x1, waiting for transfers between devices, shards(): w_columns = lax.all_gather(sliced, 'rep', axis=0, tiled=True)  121 us
    reduce_scatter x1, waiting for transfers between devices, shards(): lax.psum_scatter(jnp.dot(context, w_rows, preferred_element_type=jnp.floa...  77.6 us
    all_gather x1, waiting for transfers between devices, shards(): w_rows = lax.all_gather(out_sliced, 'rep', axis=1, tiled=True)  42.1 us
    all_to_all x1, blocking collectives, shards(): lax.all_to_all(packed, 'tp', split_axis=1, concat_axis=0, tiled=True)  28 us
    dot_general x1, matrix products, shards(): projected = jnp.dot(normed, w_columns, preferred_element_type=jnp.float32)  25.2 us
    all_to_all x1, blocking collectives, shards(): lax.all_to_all(w_out, 'tp', split_axis=0, concat_axis=1, tiled=True)  19.8 us
    convert_element_type x1, other arithmetic, shards(): floats = hidden_in.astype(jnp.float32)  18.7 us
    dot_general x1, matrix products, shards(): jnp.dot(context, w_rows, preferred_element_type=jnp.float32)  14.9 us
  transfers between devices with their start and end apart: 3, of which 3 were waited for; matrix products, arithmetic and copies ran while one was open for 22% of the time, Pallas kernels for 0%

commit v1 on v0

v1 whole, which is shorter than its diff:
```python
import jax
import jax.numpy as jnp
from jax import lax
from jax.experimental import pallas as pl
from jax.experimental.pallas import tpu as pltpu
from jax.sharding import Mesh
from jax.sharding import PartitionSpec as P

H = 64
KVH = 8
HD = 128

theta_base = 1000000.0
eps_norm = 1e-06

TP = ("zl", "y", "c")
LOG2E = 1.4426950408889634


def shift(value, axis, by):
    size = lax.axis_size(axis)
    return lax.ppermute(value, axis, [(i, (i + by) % size) for i in range(size)])


def doc_starts(lengths, count):
    places = jnp.arange(count, dtype=jnp.int32)
    ends = jnp.cumsum(lengths)
    after = places[:, None] >= ends[None, :]
    return jnp.sum(jnp.where(after, lengths[None, :], 0), axis=1)


def gather_rep(own):
    half = own.shape[0] // 2
    got = {(0, 0): (own,), (0, 1): (shift(own, "zh", 1),)}
    for dz in (0, 1):
        mine = got[0, dz][0]
        ahead, behind = shift(mine, "x", 1), shift(mine, "x", -1)
        got[1, dz], got[3, dz] = (ahead,), (behind,)
        got[2, dz] = (shift(ahead[:half], "x", 1), shift(behind[half:], "x", -1))
    return got


def attention_kernel(start_ref, query_ref, key_ref, value_ref, cos_ref, sin_ref, out_ref, *, block, span):
    count = query_ref.shape[0]
    scale = HD ** (-0.5) * LOG2E
    for number in range(count // block):
        begin = number * block
        low = max(0, begin + block - span)
        rows = query_ref[begin : begin + block, :]
        turned = rows * cos_ref[begin : begin + block, :] + pltpu.roll(rows, HD // 2, 1) * sin_ref[begin : begin + block, :]
        scores = lax.dot_general(
            turned.astype(jnp.bfloat16),
            key_ref[low : begin + block, :],
            (((1,), (1,)), ((), ())),
            preferred_element_type=jnp.float32,
        )
        width = begin + block - low
        row_at = begin + lax.broadcasted_iota(jnp.int32, (block, width), 0)
        key_at = low + lax.broadcasted_iota(jnp.int32, (block, width), 1)
        allowed = (key_at >= start_ref[begin : begin + block, :]) & (key_at <= row_at)
        scores = jnp.where(allowed, scores, -1e30)
        top = jnp.max(scores, axis=-1, keepdims=True)
        weights = jnp.exp2((scores - top) * scale)
        probs = (weights / jnp.sum(weights, axis=-1, keepdims=True)).astype(jnp.bfloat16)
        blended = jnp.dot(probs, value_ref[low : begin + block, :], preferred_element_type=jnp.float32)
        out_ref[begin : begin + block, :] = blended.astype(jnp.bfloat16)


def attend(query, key, value, starts, cosine, sine):
    count, width = query.shape
    body = lambda *refs: attention_kernel(*refs, block=256, span=768)
    whole = pl.BlockSpec((count, HD), lambda h: (0, 0))
    head = pl.BlockSpec((count, HD), lambda h: (0, h))
    return pl.pallas_call(
        body,
        grid=(width // HD,),
        in_specs=[pl.BlockSpec((count, 1), lambda h: (0, 0)), head, whole, whole, whole, whole],
        out_specs=head,
        out_shape=jax.ShapeDtypeStruct((count, width), jnp.bfloat16),
        compiler_params=pltpu.CompilerParams(vmem_limit_bytes=32 * 1024 * 1024),
    )(starts[:, None], query, key, value, cosine, sine)


def shards(hidden_in, norm_gain, w_query, w_keyval, w_out, doc_lengths):
    tp_count = lax.axis_size(TP)
    token_count, width = hidden_in.shape
    core, at_y, at_zl = lax.axis_index("c"), lax.axis_index("y"), lax.axis_index("zl")
    at_x, at_zh = lax.axis_index("x"), lax.axis_index("zh")
    rows_here = w_query.shape[0]
    query_width = w_query.shape[1] // tp_count

    query_part = w_query.reshape(rows_here, tp_count, query_width)
    keyval_part = w_keyval.reshape(rows_here, 2, KVH, HD).transpose(0, 2, 1, 3).reshape(rows_here, tp_count, HD)
    packed = jnp.concatenate([query_part, keyval_part], axis=2).reshape(rows_here, -1)
    sliced = lax.all_to_all(packed, TP, split_axis=1, concat_axis=0, tiled=True)

    columns_here = w_out.shape[1]
    turned = w_out.T.reshape(columns_here, 2, 4, -1)
    by_y = lax.all_to_all(turned, "y", split_axis=2, concat_axis=0, tiled=True)
    by_y = by_y.reshape(4, columns_here, -1)
    keep = lax.dynamic_slice_in_dim(by_y, core * 2, 2, 0)
    give = lax.dynamic_slice_in_dim(by_y, (1 - core) * 2, 2, 0)
    come = shift(give, "c", 1)
    out_own = jnp.where(core == 0, jnp.stack([keep, come], 1), jnp.stack([come, keep], 1))
    out_own = out_own.reshape(4 * columns_here, -1)

    floats = hidden_in.astype(jnp.float32)
    power = jnp.mean(floats * floats, axis=-1, keepdims=True)
    normed = (floats * lax.rsqrt(power + eps_norm) * norm_gain[None, :]).astype(jnp.bfloat16)

    got = gather_rep(sliced)
    chunk = sliced.shape[0]
    projected = None
    for (dx, dz), pieces in got.items():
        rep_from = ((at_x - dx) % 4) * 2 + (at_zh - dz) % 2
        begin = rep_from * chunk
        for piece in pieces:
            part = lax.dynamic_slice_in_dim(normed, begin, piece.shape[0], 1)
            term = jnp.dot(part, piece, preferred_element_type=jnp.float32)
            projected = term if projected is None else projected + term
            begin = begin + piece.shape[0]

    starts = doc_starts(doc_lengths[0], token_count)
    positions = jnp.arange(token_count, dtype=jnp.int32) - starts
    half = HD // 2
    freqs = theta_base ** (-(jnp.arange(half, dtype=jnp.float32) * 2.0 / HD))
    angles = positions.astype(jnp.float32)[:, None] * freqs[None, :]
    cosine, sine = jnp.cos(angles), jnp.sin(angles)
    cosine = jnp.concatenate([cosine, cosine], axis=1)
    sine = jnp.concatenate([-sine, sine], axis=1)
    keyval = projected[:, query_width:]
    flipped = jnp.concatenate([keyval[:, half:], keyval[:, :half]], axis=1)
    own_keyval = jnp.where(core == 0, keyval * cosine + flipped * sine, keyval).astype(jnp.bfloat16)
    other_keyval = shift(own_keyval, "c", 1)
    key = jnp.where(core == 0, own_keyval, other_keyval)
    value = jnp.where(core == 0, other_keyval, own_keyval)
    context = attend(projected[:, :query_width], key, value, starts, cosine, sine)

    by_token = context.reshape(2, 4, 2, -1, query_width)
    mine = lax.dynamic_index_in_dim(by_token, core, 2, keepdims=False)
    theirs = lax.dynamic_index_in_dim(by_token, 1 - core, 2, keepdims=False)
    from_core = shift(theirs, "c", 1)
    from_chip = shift(mine, "zl", 1)
    from_both = lax.ppermute(theirs, ("zl", "c"), [(i, 3 - i) for i in range(4)])
    here = jnp.where(core == 0, jnp.stack([mine, from_core], 3), jnp.stack([from_core, mine], 3))
    there = jnp.where(core == 0, jnp.stack([from_chip, from_both], 3), jnp.stack([from_both, from_chip], 3))
    gathered = jnp.where(at_zl == 0, jnp.stack([here, there], 3), jnp.stack([there, here], 3))
    gathered = gathered.reshape(token_count // 2, -1)

    got = gather_rep(out_own)
    slices = [jnp.concatenate(got[d], 0) if len(got[d]) > 1 else got[d][0] for d in sorted(got)]
    mine_all = jnp.stack(slices, 0)
    other_all = shift(mine_all, "c", 1)
    both = jnp.where(core == 0, jnp.stack([mine_all, other_all], 1), jnp.stack([other_all, mine_all], 1))
    both = both.reshape(-1, both.shape[-1])
    partial = lax.dot_general(gathered, both, (((1,), (1,)), ((), ())), preferred_element_type=jnp.float32)
    partial = partial.astype(jnp.bfloat16).reshape(2, 4, -1, partial.shape[1])

    def for_y(by):
        return lax.dynamic_index_in_dim(partial, (at_y + by) % 4, 1, keepdims=False)

    summed = for_y(0).astype(jnp.float32)
    for by in (2, 1, -1):
        summed = summed + shift(for_y(by), "y", by).astype(jnp.float32)
    keep = lax.dynamic_index_in_dim(summed, at_zl, 0, keepdims=False).astype(jnp.bfloat16)
    give = lax.dynamic_index_in_dim(summed, 1 - at_zl, 0, keepdims=False).astype(jnp.bfloat16)
    come = shift(give, "zl", 1)
    share = keep.shape[0]
    pair = jnp.where(at_zl == 0, jnp.stack([keep, come], 1), jnp.stack([come, keep], 1))
    pair = pair.reshape(share, 2, 4, 2, -1)
    pair = jnp.take(pair, (at_x - jnp.arange(4)) % 4, axis=2)
    pair = jnp.take(pair, (at_zh - jnp.arange(2)) % 2, axis=3)
    total = pair.transpose(0, 2, 3, 1, 4).reshape(share, -1)
    own_rows = lax.dynamic_slice_in_dim(hidden_in, lax.axis_index(TP) * share, share, 0).astype(jnp.float32)
    return (own_rows + total.astype(jnp.float32)).astype(jnp.bfloat16)


def solution(mesh):
    fine = Mesh(mesh.devices.reshape(4, 2, 2, 4, 2), ("x", "zh", "zl", "y", "c"))
    rep, every = ("x", "zh"), ("x", "zh", "zl", "y", "c")
    in_specs = (P(rep, None), P(), P(every, None), P(every, None), P(None, every), P(rep, None))
    return jax.shard_map(shards, mesh=fine, in_specs=in_specs, out_specs=P(every, None), check_vma=False)
```

time: 421 us -> 402 us (0.955); the launches traced: 420 us -> 394 us
  waiting for transfers between devices: 241 us -> 183 us
  starting transfers between devices: 0.09 us -> 51 us
  blocking collectives: 47.8 us -> 0 us
  local copies, waits for them, and re-layouts: 18.2 us -> 43.2 us
  other arithmetic: 37.6 us -> 52.4 us
  between operations: 13.3 us -> 1.07 us
  Pallas kernels: 0 us -> 9.54 us
  matrix products: 60.8 us -> 53.7 us
    ppermute x0 -> x28, waiting for transfers between devices: none -> 164 us  [the longest x27 152 us: shift(): lax.ppermute(value, axis, [(i, (i + by) % size) for i in range(size)])]
    all_gather x2 -> x0, waiting for transfers between devices: 163 us -> none  [the longest x1 121 us: shards(): w_columns = lax.all_gather(sliced, 'rep', axis=0, tiled=True)]
    reduce_scatter x1 -> x0, waiting for transfers between devices: 77.6 us -> none  [shards(): lax.psum_scatter(jnp.dot(context, w_rows, preferred_element_type=jnp.floa...]
    all_to_all x2 -> x0, blocking collectives: 47.8 us -> none  [the longest x1 28 us: shards(): lax.all_to_all(packed, 'tp', split_axis=1, concat_axis=0, tiled=True)]
    ppermute x0 -> x28, starting transfers between devices: none -> 42.1 us  [the longest x27 40.6 us: shift(): lax.ppermute(value, axis, [(i, (i + by) % size) for i in range(size)])]
    all_to_all x0 -> x2, waiting for transfers between devices: none -> 19.8 us  [the longest x1 15.1 us: shards(): by_y = lax.all_to_all(turned, 'y', split_axis=2, concat_axis=0, tiled=True)]
    select_n x0 -> x10, other arithmetic: none -> 16.7 us  [the longest x1 15.4 us: shards(): jnp.where(core == 0, jnp.stack([mine_all, other_all], 1), jnp.stack([othe...]
    select_n x0 -> x5, local copies, waits for them, and re-layouts: none -> 11.8 us  [the longest x1 6.64 us: shards(): jnp.where(core == 0, jnp.stack([mine_all, other_all], 1), jnp.stack([othe...]
  transfers between devices with their start and end apart: 3 -> 30, of which waited for: 3 -> 14; matrix products, arithmetic and copies ran while one was open for 22% -> 24% of each run, Pallas kernels for 0% -> 2%
where the time goes in v1:
time: 402 us; the launch traced here: 394 us
  waiting for transfers between devices  183 us (46%)
  matrix products  53.7 us (13%)
  other arithmetic  52.4 us (13%)
  starting transfers between devices  51 us (13%)
  local copies, waits for them, and re-layouts  43.2 us (11%)
  Pallas kernels  9.54 us (2%)
    ppermute x27, waiting for transfers between devices, shift(): lax.ppermute(value, axis, [(i, (i + by) % size) for i in range(size)])  152 us
    dot_general x10, matrix products, shards(): term = jnp.dot(part, piece, preferred_element_type=jnp.float32)  41.3 us
    ppermute x27, starting transfers between devices, shift(): lax.ppermute(value, axis, [(i, (i + by) % size) for i in range(size)])  40.6 us
    select_n x1, other arithmetic, shards(): jnp.where(core == 0, jnp.stack([mine_all, other_all], 1), jnp.stack([othe...  15.4 us
    convert_element_type x1, other arithmetic, shards(): (floats * lax.rsqrt(power + eps_norm) * norm_gain[None, :]).astype(jnp.bf...  15.2 us
    all_to_all x1, waiting for transfers between devices, shards(): by_y = lax.all_to_all(turned, 'y', split_axis=2, concat_axis=0, tiled=True)  15.1 us
    dot_general x1, matrix products, shards(): lax.dot_general(gathered, both, (((1,), (1,)), ((), ())), preferred_eleme...  12.5 us
    ppermute x1, waiting for transfers between devices, shards(): lax.ppermute(theirs, ('zl', 'c'), [(i, 3 - i) for i in range(4)])  11.2 us
  transfers between devices with their start and end apart: 30, of which 14 were waited for; matrix products, arithmetic and copies ran while one was open for 24% of the time, Pallas kernels for 2%

profile of v1, /device:TPU:0, one launch (start us, length us, event | category | flops | bytes accessed | tf_op | source)
XLA Modules:
  0.0 394.5 jit_solution(6867256305164839020)
XLA Ops:
  3.6 4.5 %all-to-all-start.1 = ((bf16[64,2,4,1024]{3,1,0,2:T(2,128)(2,1)}), bf16[64,2,4,1024]{3,1,0,2:T(2,128)(2,1)S(1)}, u32[]{:S(2)}, u32[]{:S(2)}) async-start(bf16[64,2,4,1024]{3,1,0,2:T(2,128)(2,1)} %copy.118), calls=%async_computation.1 | async-start | bytes 2097152 | tf_op jit(solution)/shard_map/all_to_all | solution.py:99
  8.2 15.1 %all-to-all-done.1 = bf16[64,2,4,1024]{3,1,0,2:T(2,128)(2,1)S(1)} async-done(((bf16[64,2,4,1024]{3,1,0,2:T(2,128)(2,1)}), bf16[64,2,4,1024]{3,1,0,2:T(2,128)(2,1)S(1)}, u32[]{:S(2)}, u32[]{:S(2)}) %all-to-all-start.1) | async-done | bytes 1048608 | tf_op jit(solution)/shard_map/all_to_all | solution.py:99
  39.0 7.2 %fusion = f32[1024]{0:T(1024)S(1)} fusion(bf16[1024,8192]{1,0:T(8,128)(2,1)} %param.6), kind=kLoop, calls=%fused_computation.4 | loop fusion | flops 25164800 | bytes 16781312 | tf_op jit(solution)/shard_map/reduce_sum | solution.py:108
  46.2 4.7 %all-to-all-done = bf16[64,16,640]{2,0,1:T(8,128)(2,1)} async-done(((bf16[64,16,640]{2,0,1:T(8,128)(2,1)}), bf16[64,16,640]{2,0,1:T(8,128)(2,1)}, u32[]{:S(2)}, u32[]{:S(2)}) %all-to-all-start) | async-done | bytes 1310752 | tf_op jit(solution)/shard_map/all_to_all | solution.py:95
  54.8 18.8 %collective-permute-done.14 = bf16[256,2048]{1,0:T(8,128)(2,1)} collective-permute-done((bf16[256,2048]{1,0:T(8,128)(2,1)S(1)}, bf16[256,2048]{1,0:T(8,128)(2,1)}, u32[]{:S(2)}, u32[]{:S(2)}) %collective-permute-start.14) | collective-permute-done | bytes 1048608 | tf_op jit(solution)/shard_map/ppermute | solution.py:22
  83.6 17.9 %collective-permute-done.21 = bf16[256,2048]{1,0:T(8,128)(2,1)S(1)} collective-permute-done((bf16[256,2048]{1,0:T(8,128)(2,1)}, bf16[256,2048]{1,0:T(8,128)(2,1)S(1)}, u32[]{:S(2)}, u32[]{:S(2)}) %collective-permute-start.21) | collective-permute-done | bytes 1048608 | tf_op jit(solution)/shard_map/ppermute | solution.py:22
  105.7 6.9 %collective-permute-done.19 = bf16[128,2048]{1,0:T(8,128)(2,1)S(1)} collective-permute-done((bf16[128,2048]{1,0:T(8,128)(2,1)S(1)}, bf16[128,2048]{1,0:T(8,128)(2,1)S(1)}, u32[]{:S(2)}, u32[]{:S(2)}) %collective-permute-start.19) | collective-permute-done | bytes 524320 | tf_op jit(solution)/shard_map/ppermute | solution.py:22
  116.7 7.2 %collective-permute-done.22 = bf16[128,2048]{1,0:T(8,128)(2,1)S(1)} collective-permute-done((bf16[128,2048]{1,0:T(8,128)(2,1)S(1)}, bf16[128,2048]{1,0:T(8,128)(2,1)S(1)}, u32[]{:S(2)}, u32[]{:S(2)}) %collective-permute-start.22) | collective-permute-done | bytes 524320 | tf_op jit(solution)/shard_map/ppermute | solution.py:22
  127.4 15.2 %fusion.2 = bf16[1024,8192]{1,0:T(8,128)(2,1)} fusion(bf16[1024,8192]{1,0:T(8,128)(2,1)} %param.6, f32[8192]{0:T(1024)S(1)} %copy-done.6, f32[1024]{0:T(1024)S(1)} %add_rsqrt_fusion), kind=kLoop, calls=%fused_computation.6 | loop fusion | flops 33554432 | bytes 33591296 | tf_op jit(solution)/shard_map/convert_element_type | solution.py:109
  145.9 5.4 %fusion.15 = f32[1024,640]{1,0:T(8,128)} fusion(bf16[1024,640]{1,0:T(8,128)(2,1)} %bitcast.7, bf16[1024,8192]{1,0:T(8,128)(2,1)} %fusion.2, s32[]{:T(128)S(6)} %select_n.331), kind=kOutput, calls=%fused_computation.26 | convolution fusion | flops 1342177280 | bytes 6029316 | tf_op jit(solution)/shard_map/dot_general | solution.py:119
  160.7 5.2 %fusion.9 = f32[1024,640]{1,0:T(8,128)} fusion(bf16[1024,640]{1,0:T(8,128)(2,1)} %collective-permute-done.2, bf16[1024,8192]{1,0:T(8,128)(2,1)} %fusion.2, s32[]{:T(128)S(6)} %select_n.337), kind=kOutput, calls=%fused_computation.20 | convolution fusion | flops 1342177280 | bytes 6029316 | tf_op jit(solution)/shard_map/dot_general | solution.py:119
  165.9 4.6 %fusion.11 = f32[1024,640]{1,0:T(8,128)} fusion(bf16[1024,640]{1,0:T(8,128)(2,1)} %collective-permute-done.1, bf16[1024,8192]{1,0:T(8,128)(2,1)S(1)} %copy-done, s32[]{:T(128)S(6)} %select_n.335), kind=kOutput, calls=%fused_computation.22 | convolution fusion | flops 1342177280 | bytes 6029316 | tf_op jit(solution)/shard_map/dot_general | solution.py:119
  170.5 4.6 %fusion.13 = f32[1024,640]{1,0:T(8,128)} fusion(bf16[1024,640]{1,0:T(8,128)(2,1)} %collective-permute-done, bf16[1024,8192]{1,0:T(8,128)(2,1)S(1)} %copy-done, s32[]{:T(128)S(6)} %select_n.333), kind=kOutput, calls=%fused_computation.24 | convolution fusion | flops 1342177280 | bytes 6029316 | tf_op jit(solution)/shard_map/dot_general | solution.py:119
  176.1 23.0 %collective-permute-done.6 = bf16[1024,640]{1,0:T(8,128)(2,1)S(1)} collective-permute-done((bf16[1024,640]{1,0:T(8,128)(2,1)}, bf16[1024,640]{1,0:T(8,128)(2,1)S(1)}, u32[]{:S(2)}, u32[]{:S(2)}) %collective-permute-start.6) | collective-permute-done | bytes 1310752 | tf_op jit(solution)/shard_map/ppermute | solution.py:22
  208.9 7.7 %collective-permute-done.8 = bf16[512,640]{1,0:T(8,128)(2,1)S(1)} collective-permute-done((bf16[512,640]{1,0:T(8,128)(2,1)S(1)}, bf16[512,640]{1,0:T(8,128)(2,1)S(1)}, u32[]{:S(2)}, u32[]{:S(2)}) %collective-permute-start.8) | collective-permute-done | bytes 655392 | tf_op jit(solution)/shard_map/ppermute | solution.py:22
  225.5 9.6 %add_add_fusion = f32[1024,640]{1,0:T(8,128)S(1)} fusion(f32[1024,640]{1,0:T(8,128)} %fusion.19, f32[1024,640]{1,0:T(8,128)} %fusion.21, f32[1024,640]{1,0:T(8,128)} %fusion.7, f32[1024,640]{1,0:T(8,128)S(1)} %fusion.23, f32[1024,640]{1,0:T(8,128)} %fusion.25, f32[1024,640]{1,0:T(8,128)} %fusion.9, f32[1024,640]{1,0:T(8,128)} %fusion.11, ...), kind=kOutput, calls=%fused_computation.9 | convolution fusion | flops 1348075520 | bytes 29622276 | tf_op jit(solution)/shard_map/dot_general | solution.py:119
  240.0 9.5 %shard_map.64 = bf16[1024,512]{1,0:T(8,128)(2,1)S(1)} custom-call(s32[1024,1]{1,0:T(8,128)S(1)} %copy.116.refs_0_, f32[1024,512]{1,0:T(8,128)S(1)} %slice.58.refs_1_, bf16[1024,128]{1,0:T(8,128)(2,1)S(1)} %get-tuple-element.21.refs_2_, bf16[1024,128]{1,0:T(8,128)(2,1)S(1)} %get-tuple-element.20.refs_3_, f32[1024,128]{1,0:T(8,128)S(1)} %get-tuple-element.19.refs_4_, ...), custom_call_target="tpu_custom_call" | custom-call | tf_op jit(solution)/shard_map/pallas_call | solution.py:74
  252.3 11.2 %collective-permute-done.12 = bf16[2,4,64,512]{3,2,1,0:T(8,128)(2,1)S(1)} collective-permute-done((bf16[2,4,64,512]{3,2,1,0:T(8,128)(2,1)S(1)}, bf16[2,4,64,512]{3,2,1,0:T(8,128)(2,1)S(1)}, u32[]{:S(2)}, u32[]{:S(2)}) %collective-permute-start.12) | collective-permute-done | bytes 524320 | tf_op jit(solution)/shard_map/ppermute | solution.py:144
  263.5 11.8 %collective-permute-done.11 = bf16[2,4,64,512]{3,2,1,0:T(8,128)(2,1)S(1)} collective-permute-done((bf16[2,4,64,512]{3,2,1,0:T(8,128)(2,1)S(1)}, bf16[2,4,64,512]{3,2,1,0:T(8,128)(2,1)S(1)}, u32[]{:S(2)}, u32[]{:S(2)}) %collective-permute-start.11) | collective-permute-done | bytes 524320 | tf_op jit(solution)/shard_map/ppermute | solution.py:22
  281.1 15.4 %maximum_select_fusion = bf16[8,2,256,2048]{3,2,0,1:T(8,128)(2,1)S(1)} fusion(bf16[8,1,256,2048]{3,2,0,1:T(8,128)(2,1)} %bitcast.31, bf16[8,1,256,2048]{3,2,0,1:T(8,128)(2,1)} %bitcast.30, pred[]{:T(512)S(6)} %eq.39), kind=kLoop, calls=%fused_computation.7 | loop fusion | flops 25165824 | bytes 33554432 | tf_op jit(solution)/shard_map/jit(_where)/select_n | solution.py:154
  296.5 6.6 %copy.121 = bf16[8,2,256,2048]{3,2,1,0:T(8,128)(2,1)} copy(bf16[8,2,256,2048]{3,2,0,1:T(8,128)(2,1)S(1)} %maximum_select_fusion) | data formatting | bytes 33554432 | tf_op jit(solution)/shard_map/jit(_where)/select_n | solution.py:154
  303.1 12.5 %convolution_convert_fusion = bf16[512,4096]{1,0:T(8,128)(2,1)S(1)} fusion(bf16[512,2048]{1,0:T(8,128)(2,1)S(1)} %copy-done.3, bf16[4096,2048]{1,0:T(8,128)(2,1)} %bitcast.92), kind=kOutput, calls=%fused_computation.8 | convolution fusion | flops 8592031744 | bytes 23068672 | tf_op jit(solution)/shard_map/dot_general | solution.py:156
  323.2 42.6 %collective-permute-done.26 = bf16[2,64,4096]{2,1,0:T(8,128)(2,1)S(1)} collective-permute-done((bf16[2,64,4096]{2,1,0:T(8,128)(2,1)}, bf16[2,64,4096]{2,1,0:T(8,128)(2,1)S(1)}, u32[]{:S(2)}, u32[]{:S(2)}) %collective-permute-start.26) | collective-permute-done | bytes 1048608 | tf_op jit(solution)/shard_map/ppermute | solution.py:22
  373.5 9.6 %collective-permute-done.27 = bf16[64,4096]{1,0:T(8,128)(2,1)S(1)} collective-permute-done((bf16[64,4096]{1,0:T(8,128)(2,1)S(1)}, bf16[64,4096]{1,0:T(8,128)(2,1)S(1)}, u32[]{:S(2)}, u32[]{:S(2)}) %collective-permute-start.27) | collective-permute-done | bytes 524320 | tf_op jit(solution)/shard_map/ppermute | solution.py:22
  (134 shorter events, 116.6 us)
Async XLA Ops:
  3.6 19.6 %all-to-all-start.1 = ((bf16[64,2,4,1024]{3,1,0,2:T(2,128)(2,1)}), bf16[64,2,4,1024]{3,1,0,2:T(2,128)(2,1)S(1)}, u32[]{:S(2)}, u32[]{:S(2)}) async-start(bf16[64,2,4,1024]{3,1,0,2:T(2,128)(2,1)} %copy.118), calls=%async_computation.1 | async-start | bytes 2097152 | tf_op jit(solution)/shard_map/all_to_all | solution.py:99
  27.1 23.8 %all-to-all-start = ((bf16[64,16,640]{2,0,1:T(8,128)(2,1)}), bf16[64,16,640]{2,0,1:T(8,128)(2,1)}, u32[]{:S(2)}, u32[]{:S(2)}) async-start(bf16[64,16,640]{2,0,1:T(8,128)(2,1)} %copy.105), calls=%async_computation | async-start | bytes 2621440 | tf_op jit(solution)/shard_map/all_to_all | solution.py:95
  31.8 41.8 %collective-permute-start.14 = (bf16[256,2048]{1,0:T(8,128)(2,1)S(1)}, bf16[256,2048]{1,0:T(8,128)(2,1)}, u32[]{:S(2)}, u32[]{:S(2)}) collective-permute-start(bf16[256,2048]{1,0:T(8,128)(2,1)S(1)} %bitcast.93), channel_id=1, source_target_pairs={{0,16},{16,0},{1,17},{17,1},{2,18},{18,2},{3,19},{19,3},{4,20},{20... | collective-permute-start | bytes 3145736 | tf_op jit(solution)/shard_map/ppermute | solution.py:22
  35.8 43.8 %collective-permute-start.15 = (bf16[256,2048]{1,0:T(8,128)(2,1)S(1)}, bf16[256,2048]{1,0:T(8,128)(2,1)S(1)}, u32[]{:S(2)}, u32[]{:S(2)}) collective-permute-start(bf16[256,2048]{1,0:T(8,128)(2,1)S(1)} %bitcast.94), channel_id=1, source_target_pairs={{0,32},{32,64},{64,96},{96,0},{1,33},{33,65},{65,97},{97,1},{2,34}... | collective-permute-start | bytes 3145736 | tf_op jit(solution)/shard_map/ppermute | solution.py:22
  37.3 40.6 %collective-permute-start.18 = (bf16[256,2048]{1,0:T(8,128)(2,1)S(1)}, bf16[256,2048]{1,0:T(8,128)(2,1)S(1)}, u32[]{:S(2)}, u32[]{:S(2)}) collective-permute-start(bf16[256,2048]{1,0:T(8,128)(2,1)S(1)} %bitcast.95), channel_id=1, source_target_pairs={{0,96},{32,0},{64,32},{96,64},{1,97},{33,1},{65,33},{97,65},{2,98}... | collective-permute-start | bytes 3145736 | tf_op jit(solution)/shard_map/ppermute | solution.py:22
  50.9 106.5 %collective-permute-start = (bf16[1024,640]{1,0:T(8,128)(2,1)}, bf16[1024,640]{1,0:T(8,128)(2,1)}, u32[]{:S(2)}, u32[]{:S(2)}) collective-permute-start(bf16[1024,640]{1,0:T(8,128)(2,1)} %bitcast.7), channel_id=1, source_target_pairs={{0,16},{16,0},{1,17},{17,1},{2,18},{18,2},{3,19},{19,3},{4,20},{20... | collective-permute-start | bytes 3932168 | tf_op jit(solution)/shard_map/ppermute | solution.py:22
  73.6 30.9 %collective-permute-start.16 = (bf16[256,2048]{1,0:T(8,128)(2,1)}, bf16[256,2048]{1,0:T(8,128)(2,1)S(1)}, u32[]{:S(2)}, u32[]{:S(2)}) collective-permute-start(bf16[256,2048]{1,0:T(8,128)(2,1)} %collective-permute-done.14), channel_id=1, source_target_pairs={{0,32},{32,64},{64,96},{96,0},{1,33},{33,65},{65,97},{97,1},{2,34}... | collective-permute-start | bytes 3145736 | tf_op jit(solution)/shard_map/ppermute | solution.py:22
  75.1 26.3 %collective-permute-start.21 = (bf16[256,2048]{1,0:T(8,128)(2,1)}, bf16[256,2048]{1,0:T(8,128)(2,1)S(1)}, u32[]{:S(2)}, u32[]{:S(2)}) collective-permute-start(bf16[256,2048]{1,0:T(8,128)(2,1)} %collective-permute-done.14), channel_id=1, source_target_pairs={{0,96},{32,0},{64,32},{96,64},{1,97},{33,1},{65,33},{97,65},{2,98}... | collective-permute-start | bytes 3145736 | tf_op jit(solution)/shard_map/ppermute | solution.py:22
  78.0 34.7 %collective-permute-start.19 = (bf16[128,2048]{1,0:T(8,128)(2,1)S(1)}, bf16[128,2048]{1,0:T(8,128)(2,1)S(1)}, u32[]{:S(2)}, u32[]{:S(2)}) collective-permute-start(bf16[128,2048]{1,0:T(8,128)(2,1)S(1)} %slice.63), channel_id=1, source_target_pairs={{0,96},{32,0},{64,32},{96,64},{1,97},{33,1},{65,33},{97,65},{2,98}... | collective-permute-start | bytes 1572872 | tf_op jit(solution)/shard_map/ppermute | solution.py:22
  79.6 36.0 %collective-permute-start.17 = (bf16[128,2048]{1,0:T(8,128)(2,1)S(1)}, bf16[128,2048]{1,0:T(8,128)(2,1)S(1)}, u32[]{:S(2)}, u32[]{:S(2)}) collective-permute-start(bf16[128,2048]{1,0:T(8,128)(2,1)S(1)} %slice.62), channel_id=1, source_target_pairs={{0,32},{32,64},{64,96},{96,0},{1,33},{33,65},{65,97},{97,1},{2,34}... | collective-permute-start | bytes 1572872 | tf_op jit(solution)/shard_map/ppermute | solution.py:22
  101.5 22.4 %collective-permute-start.22 = (bf16[128,2048]{1,0:T(8,128)(2,1)S(1)}, bf16[128,2048]{1,0:T(8,128)(2,1)S(1)}, u32[]{:S(2)}, u32[]{:S(2)}) collective-permute-start(bf16[128,2048]{1,0:T(8,128)(2,1)S(1)} %slice.65), channel_id=1, source_target_pairs={{0,96},{32,0},{64,32},{96,64},{1,97},{33,1},{65,33},{97,65},{2,98}... | collective-permute-start | bytes 1572872 | tf_op jit(solution)/shard_map/ppermute | solution.py:22
  104.5 19.4 %collective-permute-start.20 = (bf16[128,2048]{1,0:T(8,128)(2,1)S(1)}, bf16[128,2048]{1,0:T(8,128)(2,1)S(1)}, u32[]{:S(2)}, u32[]{:S(2)}) collective-permute-start(bf16[128,2048]{1,0:T(8,128)(2,1)S(1)} %slice.64), channel_id=1, source_target_pairs={{0,32},{32,64},{64,96},{96,0},{1,33},{33,65},{65,97},{97,1},{2,34}... | collective-permute-start | bytes 1572872 | tf_op jit(solution)/shard_map/ppermute | solution.py:22
  112.7 38.6 %collective-permute-start.2 = (bf16[1024,640]{1,0:T(8,128)(2,1)}, bf16[1024,640]{1,0:T(8,128)(2,1)}, u32[]{:S(2)}, u32[]{:S(2)}) collective-permute-start(bf16[1024,640]{1,0:T(8,128)(2,1)} %bitcast.7), channel_id=1, source_target_pairs={{0,96},{32,0},{64,32},{96,64},{1,97},{33,1},{65,33},{97,65},{2,98}... | collective-permute-start | bytes 3932168 | tf_op jit(solution)/shard_map/ppermute | solution.py:22
  115.6 40.6 %collective-permute-start.1 = (bf16[1024,640]{1,0:T(8,128)(2,1)}, bf16[1024,640]{1,0:T(8,128)(2,1)}, u32[]{:S(2)}, u32[]{:S(2)}) collective-permute-start(bf16[1024,640]{1,0:T(8,128)(2,1)} %bitcast.7), channel_id=1, source_target_pairs={{0,32},{32,64},{64,96},{96,0},{1,33},{33,65},{65,97},{97,1},{2,34}... | collective-permute-start | bytes 3932168 | tf_op jit(solution)/shard_map/ppermute | solution.py:22
  127.2 153.9 %collective-permute-start.23 = (bf16[8,256,2048]{2,1,0:T(8,128)(2,1)}, bf16[8,256,2048]{2,1,0:T(8,128)(2,1)}, u32[]{:S(2)}, u32[]{:S(2)}) collective-permute-start(bf16[8,256,2048]{2,1,0:T(8,128)(2,1)} %bitcast_dynamic-update-slice_fusion), channel_id=1, source_target_pairs={{0,1},{1,0},{2,3},{3,2},{4,5},{5,4},{6,7},{7,6},{8,9},{9,8},{10,11... | collective-permute-start | bytes 25165832 | tf_op jit(solution)/shard_map/ppermute | solution.py:22
  153.2 21.9 %collective-permute-start.4 = (bf16[512,640]{1,0:T(8,128)(2,1)S(1)}, bf16[512,640]{1,0:T(8,128)(2,1)S(1)}, u32[]{:S(2)}, u32[]{:S(2)}) collective-permute-start(bf16[512,640]{1,0:T(8,128)(2,1)S(1)} %slice.55), channel_id=1, source_target_pairs={{0,96},{32,0},{64,32},{96,64},{1,97},{33,1},{65,33},{97,65},{2,98}... | collective-permute-start | bytes 1966088 | tf_op jit(solution)/shard_map/ppermute | solution.py:22
  157.4 45.4 %collective-permute-start.3 = (bf16[512,640]{1,0:T(8,128)(2,1)S(1)}, bf16[512,640]{1,0:T(8,128)(2,1)S(1)}, u32[]{:S(2)}, u32[]{:S(2)}) collective-permute-start(bf16[512,640]{1,0:T(8,128)(2,1)S(1)} %slice.54), channel_id=1, source_target_pairs={{0,32},{32,64},{64,96},{96,0},{1,33},{33,65},{65,97},{97,1},{2,34}... | collective-permute-start | bytes 1966088 | tf_op jit(solution)/shard_map/ppermute | solution.py:22
  157.5 41.6 %collective-permute-start.6 = (bf16[1024,640]{1,0:T(8,128)(2,1)}, bf16[1024,640]{1,0:T(8,128)(2,1)S(1)}, u32[]{:S(2)}, u32[]{:S(2)}) collective-permute-start(bf16[1024,640]{1,0:T(8,128)(2,1)} %collective-permute-done), channel_id=1, source_target_pairs={{0,96},{32,0},{64,32},{96,64},{1,97},{33,1},{65,33},{97,65},{2,98}... | collective-permute-start | bytes 3932168 | tf_op jit(solution)/shard_map/ppermute | solution.py:22
  160.7 44.6 %collective-permute-start.5 = (bf16[1024,640]{1,0:T(8,128)(2,1)}, bf16[1024,640]{1,0:T(8,128)(2,1)S(1)}, u32[]{:S(2)}, u32[]{:S(2)}) collective-permute-start(bf16[1024,640]{1,0:T(8,128)(2,1)} %collective-permute-done), channel_id=1, source_target_pairs={{0,32},{32,64},{64,96},{96,0},{1,33},{33,65},{65,97},{97,1},{2,34}... | collective-permute-start | bytes 3932168 | tf_op jit(solution)/shard_map/ppermute | solution.py:22
  251.2 24.1 %collective-permute-start.11 = (bf16[2,4,64,512]{3,2,1,0:T(8,128)(2,1)S(1)}, bf16[2,4,64,512]{3,2,1,0:T(8,128)(2,1)S(1)}, u32[]{:S(2)}, u32[]{:S(2)}) collective-permute-start(bf16[2,4,64,512]{3,2,1,0:T(8,128)(2,1)S(1)} %get-tuple-element.17), channel_id=1, source_target_pairs={{0,8},{8,0},{1,9},{9,1},{2,10},{10,2},{3,11},{11,3},{4,12},{12,4},... | collective-permute-start | bytes 1572872 | tf_op jit(solution)/shard_map/ppermute | solution.py:22
  252.0 23.5 %collective-permute-start.10 = (bf16[2,4,64,512]{3,2,1,0:T(8,128)(2,1)S(1)}, bf16[2,4,64,512]{3,2,1,0:T(8,128)(2,1)S(1)}, u32[]{:S(2)}, u32[]{:S(2)}) collective-permute-start(bf16[2,4,64,512]{3,2,1,0:T(8,128)(2,1)S(1)} %get-tuple-element.18), channel_id=1, source_target_pairs={{0,1},{1,0},{2,3},{3,2},{4,5},{5,4},{6,7},{7,6},{8,9},{9,8},{10,11... | collective-permute-start | bytes 1572872 | tf_op jit(solution)/shard_map/ppermute | solution.py:22
  317.9 47.9 %collective-permute-start.26 = (bf16[2,64,4096]{2,1,0:T(8,128)(2,1)}, bf16[2,64,4096]{2,1,0:T(8,128)(2,1)S(1)}, u32[]{:S(2)}, u32[]{:S(2)}) collective-permute-start(bf16[2,64,4096]{2,1,0:T(8,128)(2,1)} %get-tuple-element.8), channel_id=1, source_target_pairs={{0,6},{2,0},{4,2},{6,4},{1,7},{3,1},{5,3},{7,5},{8,14},{10,8},{12,... | collective-permute-start | bytes 3145736 | tf_op jit(solution)/shard_map/ppermute | solution.py:22
  320.9 48.0 %collective-permute-start.25 = (bf16[2,64,4096]{2,1,0:T(8,128)(2,1)S(1)}, bf16[2,64,4096]{2,1,0:T(8,128)(2,1)}, u32[]{:S(2)}, u32[]{:S(2)}) collective-permute-start(bf16[2,64,4096]{2,1,0:T(8,128)(2,1)S(1)} %get-tuple-element.9), channel_id=1, source_target_pairs={{0,2},{2,4},{4,6},{6,0},{1,3},{3,5},{5,7},{7,1},{8,10},{10,12},{12... | collective-permute-start | bytes 3145736 | tf_op jit(solution)/shard_map/ppermute | solution.py:22
  320.9 48.0 %collective-permute-start.24 = (bf16[2,64,4096]{2,1,0:T(8,128)(2,1)S(1)}, bf16[2,64,4096]{2,1,0:T(8,128)(2,1)}, u32[]{:S(2)}, u32[]{:S(2)}) collective-permute-start(bf16[2,64,4096]{2,1,0:T(8,128)(2,1)S(1)} %get-tuple-element.7), channel_id=1, source_target_pairs={{0,4},{2,6},{4,0},{6,2},{1,5},{3,7},{5,1},{7,3},{8,12},{10,14},{12... | collective-permute-start | bytes 3145736 | tf_op jit(solution)/shard_map/ppermute | solution.py:22
  (14 other events, 137.3 us)
